TPU v7x, 32 devices: a whole 2x2x4 slice. The times are simulated.
32 devices in a mesh: expert: 4 (over z), rep: 4 (over y, core), hid: 2 (over x).
Axes of the slice: x: 2, y: 2, z: 4, core: 2. Of those that a mesh axis runs over, the one named last changes fastest.
Arguments:
- tokens: bfloat16 [64, 6144], P(('expert', 'hid'), 'rep'), may hold values from -6 to 6
- norm_gain: float32 [6144], P('rep'), may hold values from 0.25 to 1.75
- expert_ids: int32 [64, 2], P(('expert', 'hid')), may hold values from 0 to 3, as said below
- slot_ids: int32 [64, 2], P(('expert', 'hid')), may hold values from 0 to 4, as said below
- w_gate: bfloat16 [4, 6144, 8192], P('expert', 'rep', 'hid'), may hold values from -0.078125 to 0.078125
- w_up: bfloat16 [4, 6144, 8192], P('expert', 'rep', 'hid'), may hold values from -0.078125 to 0.078125
- grad_gate: bfloat16 [4, 40, 8192], P('expert', None, 'hid'), may hold values from -1.1953125 to 1.1953125
- grad_up: bfloat16 [4, 40, 8192], P('expert', None, 'hid'), may hold values from -1.1953125 to 1.1953125
Outputs:
- grad_w_gate: bfloat16 [4, 6144, 8192], P('expert', 'rep', 'hid')
- grad_w_up: bfloat16 [4, 6144, 8192], P('expert', 'rep', 'hid')
- grad_tokens: bfloat16 [64, 6144], P(('expert', 'hid'), 'rep')
Inputs may be any that keep to these rules, and one draw needn't show every extreme that they name: `expert_ids`: each token names two different experts; among the 8 tokens of one block, no expert is named more than 5 times and some expert exactly 5 times. Within one block of 8 tokens, the pairs (expert_ids[t, k], slot_ids[t, k]) are all different.
All inputs are finite; a program needn't handle non-finite values.
Results may differ from a plain program's by a relative error of at most 0.0049.
Values may be sent and summed in bfloat16 or wider, within the bound.
A program may use at most 128 MiB of HBM per device.

v0:
```python
import jax
import jax.numpy as jnp
from jax import lax
from jax.sharding import PartitionSpec as P

D = 6144


def feature_total(partial_value):
    return lax.psum(partial_value, "rep")


def on_device(tokens, norm_gain, expert_ids, slot_ids, w_gate, w_up, grad_gate, grad_up):
    groups = lax.axis_size("expert")
    block_tokens = tokens.shape[0]
    slot_count = 5 * block_tokens // (2 * groups)
    values = tokens.astype(jnp.float32)
    square_sums = feature_total(jnp.sum(values * values, axis=1))
    inverse_rms = lax.rsqrt(square_sums / D + 1e-05)[:, None]
    scaled_in = values * inverse_rms
    normed = (scaled_in * norm_gain).astype(jnp.bfloat16)
    slot_code = expert_ids * slot_count + slot_ids
    codes_all = jnp.arange(groups * slot_count, dtype=jnp.int32)
    onehot = (
        (slot_code[:, 0][None, :] == codes_all[:, None])
        | (slot_code[:, 1][None, :] == codes_all[:, None])
    ).astype(jnp.bfloat16)
    feat_width = normed.shape[1]
    outgoing = (
        jnp.dot(onehot, normed, preferred_element_type=jnp.float32)
        .astype(jnp.bfloat16)
        .reshape(groups, slot_count, feat_width)
    )
    arrived = lax.all_to_all(outgoing, "expert", split_axis=0, concat_axis=0, tiled=True)
    own_rows = arrived.reshape(groups * slot_count, feat_width)
    gate_cot = grad_gate[0]
    up_cot = grad_up[0]
    row_contract = (((0,), (0,)), ((), ()))
    gathered = lax.all_gather(own_rows, "hid", axis=0, tiled=True)
    gate_part = gate_cot
    up_part = up_cot
    new_gate = lax.dot_general(
        gathered, gate_part, row_contract, preferred_element_type=jnp.float32
    )
    new_up = lax.dot_general(gathered, up_part, row_contract, preferred_element_type=jnp.float32)
    unit_contract = (((1,), (1,)), ((), ()))
    gate_part = gate_cot
    up_part = up_cot
    first_term = lax.dot_general(
        gate_part, w_gate[0], unit_contract, preferred_element_type=jnp.float32
    )
    summed = lax.psum_scatter(
        first_term
        + lax.dot_general(up_part, w_up[0], unit_contract, preferred_element_type=jnp.float32),
        "hid",
        scatter_dimension=0,
        tiled=True,
    )
    returned_rows = lax.all_to_all(
        summed.astype(jnp.bfloat16).reshape(groups, slot_count, feat_width),
        "expert",
        split_axis=0,
        concat_axis=0,
        tiled=True,
    )
    normed_grad = jnp.dot(
        onehot.T,
        returned_rows.reshape(groups * slot_count, feat_width),
        preferred_element_type=jnp.float32,
    )
    scaled = normed_grad * norm_gain
    dotted = feature_total(jnp.sum(scaled * scaled_in, axis=1)) / D
    grad_tokens = (inverse_rms * (scaled - scaled_in * dotted[:, None])).astype(jnp.bfloat16)
    return (new_gate.astype(jnp.bfloat16)[None], new_up.astype(jnp.bfloat16)[None], grad_tokens)


def solution(mesh):
    placed = (
        P(("expert", "hid"), "rep"),
        P("rep"),
        P(("expert", "hid"), None),
        P(("expert", "hid"), None),
        P("expert", "rep", "hid"),
        P("expert", "rep", "hid"),
        P("expert", None, "hid"),
        P("expert", None, "hid"),
    )
    return jax.shard_map(
        on_device,
        mesh=mesh,
        in_specs=placed,
        out_specs=(
            P("expert", "rep", "hid"),
            P("expert", "rep", "hid"),
            P(("expert", "hid"), "rep"),
        ),
        check_vma=False,
    )
```

profile of v0, /device:TPU:0, one launch (start us, length us, event | category | flops | bytes accessed | tf_op | source)
XLA Modules:
  0.0 72.6 jit_solution(14137795766581464414)
XLA Ops:
  0.6 0.0 copy-start
  0.7 1.0 %fusion.22 = f32[8]{0:T(128)S(1)} fusion(bf16[8,1536]{1,0:T(8,128)(2,1)} %param.8), kind=kLoop, calls=%fused_computation.26 | loop fusion | flops 36856 | bytes 24608 | tf_op jit(solution)/shard_map/reduce_sum | solution.py:18
  1.7 0.0 copy-start.6
  1.7 0.0 copy-start.3
  1.7 0.0 copy-start.7
  1.7 8.9 %fusion.3 = f32[40,1536]{1,0:T(8,128)S(1)} fusion(bf16[1,1536,4096]{2,1,0:T(8,128)(2,1)} %param.13, bf16[1,40,4096]{2,1,0:T(8,128)(2,1)S(1)} %copy-done), kind=kOutput, calls=%fused_computation.4 | convolution fusion | flops 503316480 | bytes 13156352 | tf_op jit(solution)/shard_map/dot_general | solution.py:54
  10.7 3.9 %fusion.7 = f32[40,1536]{1,0:T(8,128)S(1)} fusion(f32[40,1536]{1,0:T(8,128)S(1)} %fusion.3, bf16[1,1536,4096]{2,1,0:T(8,128)(2,1)S(1)} %copy-done.1, bf16[1,40,4096]{2,1,0:T(8,128)(2,1)S(1)} %copy-done.2), kind=kOutput, calls=%fused_computation.8 | convolution fusion | flops 503377920 | bytes 13402112 | tf_op jit(solution)/shard_map/dot_general | solution.py:49
  14.6 9.9 %fusion = f32[24,1536]{1,0:T(8,128)S(1)} fusion(f32[40,1536]{1,0:T(8,128)S(1)} %fusion.7), kind=kCustom, calls=%all-reduce-scatter | all-reduce-scatter fusion | flops 73729 | bytes 393728
  24.5 2.2 %collective-permute-start = (bf16[4,1536]{1,0:T(4,128)(2,1)S(1)}, bf16[4,1536]{1,0:T(4,128)(2,1)S(1)}, u32[]{:S(2)}, u32[]{:S(2)}) collective-permute-start(bf16[4,1536]{1,0:T(4,128)(2,1)S(1)} %slice.8), channel_id=1, source_target_pairs={{0,1},{2,3},{4,5},{6,7},{8,9},{10,11},{12,13},{14,15},{16,17},{18,... | collective-permute-start | bytes 36872
  26.7 5.7 %psum.14 = f32[8]{0:T(128)S(1)} all-reduce(f32[8]{0:T(128)S(1)} %fusion.22), channel_id=1, replica_groups=mesh['expert'=4,'rep'=4,'hid'=2] {'rep'}, use_global_device_ids=true, to_apply=%region_1.0 | all-reduce | flops 8 | bytes 64 | tf_op jit(solution)/shard_map/psum | solution.py:10
  32.4 0.2 convolution_convert_fusion.2
  32.6 0.7 reshape.23
  33.3 5.1 %all-to-all-start = ((bf16[4,5,1536]{2,1,0:T(8,128)(2,1)}), bf16[4,5,1536]{2,1,0:T(8,128)(2,1)S(1)}, u32[]{:S(2)}, u32[]{:S(2)}) async-start(bf16[4,5,1536]{2,1,0:T(8,128)(2,1)} %reshape.23), calls=%async_computation | async-start | bytes 196608 | tf_op jit(solution)/shard_map/all_to_all | solution.py:34
  38.4 0.6 dynamic-slice.4
  39.7 0.2 concatenate
  39.9 0.7 reshape.25
  40.6 3.7 %all-to-all-done = bf16[4,5,1536]{2,1,0:T(8,128)(2,1)S(1)} async-done(((bf16[4,5,1536]{2,1,0:T(8,128)(2,1)}), bf16[4,5,1536]{2,1,0:T(8,128)(2,1)S(1)}, u32[]{:S(2)}, u32[]{:S(2)}) %all-to-all-start) | async-done | bytes 61472 | tf_op jit(solution)/shard_map/all_to_all | solution.py:34
  44.2 3.3 %all-to-all-start.1 = ((bf16[4,5,1536]{2,1,0:T(8,128)(2,1)}), bf16[4,5,1536]{2,1,0:T(8,128)(2,1)S(1)}, u32[]{:S(2)}, u32[]{:S(2)}) async-start(bf16[4,5,1536]{2,1,0:T(8,128)(2,1)} %reshape.25), calls=%async_computation.1 | async-start | bytes 196608 | tf_op jit(solution)/shard_map/all_to_all | solution.py:59
  47.6 5.0 %all-gather = bf16[2,20,1536]{2,1,0:T(8,128)(2,1)S(1)} all-gather(bf16[1,20,1536]{2,1,0:T(8,128)(2,1)S(1)} %reshape.27), channel_id=1, replica_groups=mesh['expert'=4,'rep'=4,'hid'=2] {'hid'}, dimensions={0}, use_global_device_ids=true | all-gather | bytes 184320 | tf_op jit(solution)/shard_map/all_gather | solution.py:39
  52.7 6.6 %fusion.2 = bf16[1,1536,4096]{2,1,0:T(8,128)(2,1)} fusion(bf16[40,1536]{1,0:T(8,128)(2,1)S(1)} %reshape.28, bf16[1,40,4096]{2,1,0:T(8,128)(2,1)S(1)} %copy-done), kind=kOutput, calls=%fused_computation.3 | convolution fusion | flops 509607936 | bytes 13033472 | tf_op jit(solution)/shard_map/dot_general | solution.py:45
  59.3 6.6 %fusion.1 = bf16[1,1536,4096]{2,1,0:T(8,128)(2,1)} fusion(bf16[40,1536]{1,0:T(8,128)(2,1)S(1)} %reshape.28, bf16[1,40,4096]{2,1,0:T(8,128)(2,1)S(1)} %copy-done.2), kind=kOutput, calls=%fused_computation.2 | convolution fusion | flops 509607936 | bytes 13033472 | tf_op jit(solution)/shard_map/dot_general | solution.py:42
  65.9 0.3 fusion.18
  66.3 5.7 %psum.15 = f32[8]{0:T(128)S(1)} all-reduce(f32[8]{0:T(128)S(1)} %get-tuple-element.5), channel_id=1, replica_groups=mesh['expert'=4,'rep'=4,'hid'=2] {'rep'}, use_global_device_ids=true, to_apply=%region_4.0 | all-reduce | flops 8 | bytes 64 | tf_op jit(solution)/shard_map/psum | solution.py:10
  71.9 0.7 fusion.21
  (23 shorter events, 0.2 us)
Async XLA Ops:
  0.6 1.1 %copy-start = (bf16[1,40,4096]{2,1,0:T(8,128)(2,1)S(1)}, bf16[1,40,4096]{2,1,0:T(8,128)(2,1)}, u32[]{:S(2)}) copy-start(bf16[1,40,4096]{2,1,0:T(8,128)(2,1)} %param.15) | copy-start | bytes 983044
  0.6 10.0 %copy-start.2 = (bf16[1,40,4096]{2,1,0:T(8,128)(2,1)S(1)}, bf16[1,40,4096]{2,1,0:T(8,128)(2,1)}, u32[]{:S(2)}) copy-start(bf16[1,40,4096]{2,1,0:T(8,128)(2,1)} %param.14) | copy-start | bytes 983044
  0.7 10.0 %copy-start.1 = (bf16[1,1536,4096]{2,1,0:T(8,128)(2,1)S(1)}, bf16[1,1536,4096]{2,1,0:T(8,128)(2,1)}, u32[]{:S(2)}) copy-start(bf16[1,1536,4096]{2,1,0:T(8,128)(2,1)} %param.12) | copy-start | bytes 37748740
  1.7 30.7 %copy-start.5 = (s32[8,2]{0,1:T(2,128)S(1)}, s32[8,2]{0,1:T(2,128)}, u32[]{:S(2)}) copy-start(s32[8,2]{0,1:T(2,128)} %param.11) | copy-start | bytes 196
  1.7 30.7 %copy-start.6 = (s32[8,2]{0,1:T(2,128)S(1)}, s32[8,2]{0,1:T(2,128)}, u32[]{:S(2)}) copy-start(s32[8,2]{0,1:T(2,128)} %param.10) | copy-start | bytes 196
  1.7 30.7 %copy-start.3 = (bf16[8,1536]{1,0:T(8,128)(2,1)S(1)}, bf16[8,1536]{1,0:T(8,128)(2,1)}, u32[]{:S(2)}) copy-start(bf16[8,1536]{1,0:T(8,128)(2,1)} %param.8) | copy-start | bytes 73732
  1.7 30.7 %copy-start.4 = (f32[1536]{0:T(1024)S(1)}, f32[1536]{0:T(1024)}, u32[]{:S(2)}) copy-start(f32[1536]{0:T(1024)} %param.9) | copy-start | bytes 18436
  1.7 36.7 %copy-start.7 = (u32[32]{0:T(128)S(1)}, u32[32]{0:T(128)}, u32[]{:S(2)}) copy-start(u32[32]{0:T(128)} %constant.16) | copy-start | bytes 388
  24.5 15.2 %collective-permute-start = (bf16[4,1536]{1,0:T(4,128)(2,1)S(1)}, bf16[4,1536]{1,0:T(4,128)(2,1)S(1)}, u32[]{:S(2)}, u32[]{:S(2)}) collective-permute-start(bf16[4,1536]{1,0:T(4,128)(2,1)S(1)} %slice.8), channel_id=1, source_target_pairs={{0,1},{2,3},{4,5},{6,7},{8,9},{10,11},{12,13},{14,15},{16,17},{18,... | collective-permute-start | bytes 36872
  33.3 11.0 %all-to-all-start = ((bf16[4,5,1536]{2,1,0:T(8,128)(2,1)}), bf16[4,5,1536]{2,1,0:T(8,128)(2,1)S(1)}, u32[]{:S(2)}, u32[]{:S(2)}) async-start(bf16[4,5,1536]{2,1,0:T(8,128)(2,1)} %reshape.23), calls=%async_computation | async-start | bytes 196608 | tf_op jit(solution)/shard_map/all_to_all | solution.py:34
  44.2 21.7 %all-to-all-start.1 = ((bf16[4,5,1536]{2,1,0:T(8,128)(2,1)}), bf16[4,5,1536]{2,1,0:T(8,128)(2,1)S(1)}, u32[]{:S(2)}, u32[]{:S(2)}) async-start(bf16[4,5,1536]{2,1,0:T(8,128)(2,1)} %reshape.25), calls=%async_computation.1 | async-start | bytes 196608 | tf_op jit(solution)/shard_map/all_to_all | solution.py:59
where the time goes:
time: 73 us; the launch traced here: 72.6 us
  matrix products  26.5 us (36%)
  blocking collectives  26.3 us (36%)
  starting transfers between devices  10.6 us (15%)
  waiting for transfers between devices  3.69 us (5%)
  local copies, waits for them, and re-layouts  2.3 us (3%)
  other arithmetic  1.72 us (2%)
  between operations  1.49 us (2%)
    psum x2, blocking collectives, feature_total(): return lax.psum(partial_value, 'rep')  11.3 us
    unnamed x1, blocking collectives  9.9 us
    dot_general x1, matrix products, on_device(): lax.dot_general(up_part, w_up[0], unit_contract, preferred_element_type=j...  8.91 us
    dot_general x1, matrix products, on_device(): lax.dot_general(gathered, up_part, row_contract, preferred_element_type=j...  6.63 us
    dot_general x1, matrix products, on_device(): lax.dot_general(gathered, gate_part, row_contract, preferred_element_type...  6.61 us
    all_to_all x1, starting transfers between devices, on_device(): lax.all_to_all(outgoing, 'expert', split_axis=0, concat_axis=0, tiled=True)  5.12 us
    all_gather x1, blocking collectives, on_device(): gathered = lax.all_gather(own_rows, 'hid', axis=0, tiled=True)  5.03 us
    dot_general x1, matrix products, on_device(): lax.dot_general(gate_part, w_gate[0], unit_contract, preferred_element_ty...  3.87 us
  transfers between devices with their start and end apart: 3, of which 1 were waited for; matrix products, arithmetic and copies ran while one was open for 22% of the time, Pallas kernels for 0%

commit v1 on v0

v1 whole, which is shorter than its diff:
```python
import functools

import jax
import jax.numpy as jnp
from jax import lax
from jax.experimental import pallas as pl
from jax.experimental.pallas import tpu as pltpu
from jax.sharding import PartitionSpec as P

EPS = 1e-05
MESH = pl.DeviceIdType.MESH
F32 = jnp.float32
BF16 = jnp.bfloat16
MIB = 1024 * 1024


def divisor_up_to(size, most, step):
    best = size
    for width in range(step, most + 1, step):
        if size % width == 0:
            best = width
    return best


def exchange_kernel(
    sizes,
    tokens_ref,
    gain_ref,
    experts_ref,
    slots_ref,
    w_gate_ref,
    w_up_ref,
    gate_ref,
    up_ref,
    rows_t_ref,
    grad_tokens_ref,
    gate_buf,
    up_buf,
    gate_pad,
    up_pad,
    outgoing,
    arrived,
    back_out,
    back_in,
    sums,
    w_sem,
    sum_send,
    sum_recv,
    row_send,
    row_recv,
    back_send,
    back_recv,
):
    groups, reps, hids, slot_count, pad, chunk, per_send, sends, model = sizes
    blocks = groups * hids
    shift = pad.bit_length() - 1
    my_e = lax.axis_index("expert")
    my_r = lax.axis_index("rep")
    my_h = lax.axis_index("hid")
    me = my_h * groups + my_e
    chunks = per_send * sends
    block_tokens, feats = tokens_ref.shape
    slot_rows = gate_ref.shape[0]

    def weight_copies(c):
        rows = pl.ds(pl.multiple_of(c * chunk, chunk), chunk)
        return (
            pltpu.make_async_copy(w_gate_ref.at[rows, :], gate_buf.at[c], w_sem.at[0, c]),
            pltpu.make_async_copy(w_up_ref.at[rows, :], up_buf.at[c], w_sem.at[1, c]),
        )

    def start_weights(c, carry):
        for copy in weight_copies(c):
            copy.start()
        return carry

    lax.fori_loop(0, chunks, start_weights, 0)

    def block_at(step):
        other = lax.rem(me + step, blocks)
        return other, (lax.rem(other, groups), my_r, lax.div(other, groups))

    def rep_at(step):
        other = lax.rem(my_r + step, reps)
        return other, (my_e, other, my_h)

    barrier = pltpu.get_barrier_semaphore()

    def greet_rep(step, carry):
        pl.semaphore_signal(barrier, inc=1, device_id=rep_at(step)[1], device_id_type=MESH)
        return carry

    def greet_block(step, carry):
        pl.semaphore_signal(barrier, inc=1, device_id=block_at(step)[1], device_id_type=MESH)
        return carry

    lax.fori_loop(1, reps, greet_rep, 0)
    lax.fori_loop(1, blocks, greet_block, 0)

    def sum_copy(turn, step, sending):
        there, where = rep_at(step if sending else reps - step)
        slot = my_r if sending else there
        return pltpu.make_async_remote_copy(
            src_ref=sums.at[turn, my_r],
            dst_ref=sums.at[turn, slot],
            send_sem=sum_send.at[turn, step],
            recv_sem=sum_recv.at[turn, slot],
            device_id=where,
            device_id_type=MESH,
        )

    def send_sums(turn):
        def go(step, carry):
            sum_copy(turn, step, True).start()
            return carry

        lax.fori_loop(1, reps, go, 0)

    def wait_sums(turn):
        def go(step, carry):
            sum_copy(turn, step, False).wait_recv()
            return carry

        lax.fori_loop(1, reps, go, 0)
        return jnp.sum(sums[turn], axis=0)[:, :1]

    values = tokens_ref[...].astype(F32)
    sums[0, my_r] = jnp.broadcast_to(
        jnp.sum(values * values, axis=1, keepdims=True), (block_tokens, 128)
    )

    wide = blocks * pad
    padded_at = lax.broadcasted_iota(jnp.int32, (wide, slot_rows), 0)
    packed_at = lax.broadcasted_iota(jnp.int32, (wide, slot_rows), 1)
    slot_at = padded_at & (pad - 1)
    spread = (
        (packed_at == (padded_at >> shift) * slot_count + slot_at) & (slot_at < slot_count)
    ).astype(F32).astype(BF16)
    gate_pad[...] = jnp.dot(spread, gate_ref[...], preferred_element_type=F32).astype(BF16)
    up_pad[...] = jnp.dot(spread, up_ref[...], preferred_element_type=F32).astype(BF16)

    code = experts_ref[...] * pad + slots_ref[...]
    code_at = lax.broadcasted_iota(jnp.int32, (groups * pad, block_tokens), 0)
    onehot = ((code[0:1, :] == code_at) | (code[1:2, :] == code_at)).astype(F32)

    pl.semaphore_wait(barrier, reps + blocks - 2)
    send_sums(0)

    def back_copy(s, step, sending):
        there, where = block_at(step if sending else blocks - step)
        slot = me if sending else there
        return pltpu.make_async_remote_copy(
            src_ref=back_out.at[s, there],
            dst_ref=back_in.at[s, slot],
            send_sem=back_send.at[s, step],
            recv_sem=back_recv.at[s, slot],
            device_id=where,
            device_id_type=MESH,
        )

    contract_last = (((1,), (1,)), ((), ()))

    def back_part(s, carry):
        for part in range(per_send):
            c = s * per_send + part
            gate_copy, up_copy = weight_copies(c)
            gate_copy.wait()
            total = lax.dot_general(
                gate_pad[...], gate_buf[c], contract_last, preferred_element_type=F32
            )
            up_copy.wait()
            total = total + lax.dot_general(
                up_pad[...], up_buf[c], contract_last, preferred_element_type=F32
            )
            back_out[s, :, :, part * chunk : (part + 1) * chunk] = total.astype(BF16).reshape(
                blocks, pad, chunk
            )

        def go(step, inner):
            back_copy(s, step, True).start()
            return inner

        lax.fori_loop(1, blocks, go, 0)
        back_in[s, me] = back_out[s, me]
        return carry

    back_part(0, 0)

    gain = gain_ref[...]
    inverse_rms = lax.rsqrt(wait_sums(0) / model + EPS)
    scaled_in = values * inverse_rms
    normed = (scaled_in * gain).astype(BF16)
    outgoing[...] = (
        jnp.dot(onehot.astype(BF16), normed, preferred_element_type=F32)
        .astype(BF16)
        .reshape(groups, pad, feats)
    )

    def row_copy(step, sending):
        there, where = block_at(step if sending else blocks - step)
        slot = me if sending else there
        return pltpu.make_async_remote_copy(
            src_ref=outgoing.at[lax.rem(there, groups)],
            dst_ref=arrived.at[slot],
            send_sem=row_send.at[step],
            recv_sem=row_recv.at[slot],
            device_id=where,
            device_id_type=MESH,
        )

    def start_rows(step, carry):
        row_copy(step, True).start()
        return carry

    lax.fori_loop(1, blocks, start_rows, 0)
    arrived[me] = outgoing[my_e]

    lax.fori_loop(1, sends, back_part, 0)

    def wait_rows(step, carry):
        row_copy(step, False).wait_recv()
        return carry

    lax.fori_loop(1, blocks, wait_rows, 0)
    rows_t_ref[...] = lax.dot_general(
        arrived[...].reshape(wide, feats),
        spread,
        (((0,), (0,)), ((), ())),
        preferred_element_type=F32,
    ).astype(BF16)

    def wait_back(s, carry):
        def go(step, inner):
            back_copy(s, step, False).wait_recv()
            return inner

        return lax.fori_loop(1, blocks, go, carry)

    lax.fori_loop(0, sends, wait_back, 0)
    pick = jnp.concatenate([onehot] * hids, axis=0).astype(BF16)
    normed_grad = jnp.concatenate(
        [
            lax.dot_general(
                pick,
                back_in[s].reshape(wide, per_send * chunk),
                (((0,), (0,)), ((), ())),
                preferred_element_type=F32,
            )
            for s in range(sends)
        ],
        axis=1,
    )
    scaled = normed_grad * gain
    sums[1, my_r] = jnp.broadcast_to(
        jnp.sum(scaled * scaled_in, axis=1, keepdims=True), (block_tokens, 128)
    )
    send_sums(1)

    def sent_rows(step, carry):
        row_copy(step, True).wait_send()
        return carry

    def sent_back(s, carry):
        def go(step, inner):
            back_copy(s, step, True).wait_send()
            return inner

        return lax.fori_loop(1, blocks, go, carry)

    lax.fori_loop(1, blocks, sent_rows, 0)
    lax.fori_loop(0, sends, sent_back, 0)
    dotted = wait_sums(1) / model
    grad_tokens_ref[...] = (inverse_rms * (scaled - scaled_in * dotted)).astype(BF16)

    def sent_sums(step, carry):
        sum_copy(0, step, True).wait_send()
        sum_copy(1, step, True).wait_send()
        return carry

    lax.fori_loop(1, reps, sent_sums, 0)


def weight_grad_kernel(
    chunk, columns, rows_t_ref, gate_ref, up_ref, gate_out, up_out, gate_buf, up_buf, sem
):
    feats = rows_t_ref.shape[0]
    width = gate_ref.shape[1]

    def out_copies(c):
        rows = pl.ds(pl.multiple_of(c * chunk, chunk), chunk)
        return (
            pltpu.make_async_copy(gate_buf.at[c], gate_out.at[rows, :], sem.at[0, c]),
            pltpu.make_async_copy(up_buf.at[c], up_out.at[rows, :], sem.at[1, c]),
        )

    def one(c, carry):
        lhs = rows_t_ref[pl.ds(pl.multiple_of(c * chunk, chunk), chunk), :]
        copies = out_copies(c)
        for cot_ref, buf, copy in ((gate_ref, gate_buf, copies[0]), (up_ref, up_buf, copies[1])):
            for at in range(0, width, columns):
                buf[c, :, at : at + columns] = jnp.dot(
                    lhs, cot_ref[:, at : at + columns], preferred_element_type=F32
                ).astype(BF16)
            copy.start()
        return carry

    lax.fori_loop(0, feats // chunk, one, 0)

    def finish(c, carry):
        for copy in out_copies(c):
            copy.wait()
        return carry

    lax.fori_loop(0, feats // chunk, finish, 0)


def on_device(model, tokens, norm_gain, expert_ids, slot_ids, w_gate, w_up, grad_gate, grad_up):
    groups, reps, hids = (lax.axis_size(name) for name in ("expert", "rep", "hid"))
    blocks = groups * hids
    block_tokens, feats = tokens.shape
    slot_count = 5 * block_tokens // (2 * groups)
    pad = max(8, 1 << (slot_count - 1).bit_length())
    width = w_gate.shape[2]
    slot_rows = grad_gate.shape[1]
    chunk = divisor_up_to(feats, 256, 128)
    chunks = feats // chunk
    per_send = 2 if chunks % 2 == 0 else 1
    sends = chunks // per_send
    vmem = pl.BlockSpec(memory_space=pltpu.VMEM)
    hbm = pl.BlockSpec(memory_space=pl.ANY)
    wide = blocks * pad
    weight_bytes = feats * width * 2
    gate_cot = grad_gate[0]
    up_cot = grad_up[0]
    rows_t, grad_tokens = pl.pallas_call(
        functools.partial(
            exchange_kernel,
            (groups, reps, hids, slot_count, pad, chunk, per_send, sends, model),
        ),
        out_shape=(
            jax.ShapeDtypeStruct((feats, slot_rows), BF16),
            jax.ShapeDtypeStruct((block_tokens, feats), BF16),
        ),
        in_specs=[vmem, vmem, vmem, vmem, hbm, hbm, vmem, vmem],
        out_specs=(vmem, vmem),
        scratch_shapes=[
            pltpu.VMEM((chunks, chunk, width), BF16),
            pltpu.VMEM((chunks, chunk, width), BF16),
            pltpu.VMEM((wide, width), BF16),
            pltpu.VMEM((wide, width), BF16),
            pltpu.VMEM((groups, pad, feats), BF16),
            pltpu.VMEM((blocks, pad, feats), BF16),
            pltpu.VMEM((sends, blocks, pad, per_send * chunk), BF16),
            pltpu.VMEM((sends, blocks, pad, per_send * chunk), BF16),
            pltpu.VMEM((2, reps, block_tokens, 128), F32),
            pltpu.SemaphoreType.DMA((2, chunks)),
            pltpu.SemaphoreType.DMA((2, reps)),
            pltpu.SemaphoreType.DMA((2, reps)),
            pltpu.SemaphoreType.DMA((blocks,)),
            pltpu.SemaphoreType.DMA((blocks,)),
            pltpu.SemaphoreType.DMA((sends, blocks)),
            pltpu.SemaphoreType.DMA((sends, blocks)),
        ],
        compiler_params=pltpu.CompilerParams(
            collective_id=0, has_side_effects=True, vmem_limit_bytes=48 * MIB
        ),
        cost_estimate=pl.CostEstimate(
            flops=4 * wide * feats * width,
            bytes_accessed=2 * weight_bytes,
            transcendentals=0,
        ),
        name="rows_and_token_grads",
    )(
        tokens,
        norm_gain.reshape(1, feats),
        expert_ids.T,
        slot_ids.T,
        w_gate[0],
        w_up[0],
        gate_cot,
        up_cot,
    )
    new_gate, new_up = pl.pallas_call(
        functools.partial(weight_grad_kernel, chunk, divisor_up_to(width, 512, 128)),
        out_shape=(
            jax.ShapeDtypeStruct((feats, width), BF16),
            jax.ShapeDtypeStruct((feats, width), BF16),
        ),
        in_specs=[vmem, vmem, vmem],
        out_specs=(hbm, hbm),
        scratch_shapes=[
            pltpu.VMEM((chunks, chunk, width), BF16),
            pltpu.VMEM((chunks, chunk, width), BF16),
            pltpu.SemaphoreType.DMA((2, chunks)),
        ],
        compiler_params=pltpu.CompilerParams(vmem_limit_bytes=48 * MIB),
        cost_estimate=pl.CostEstimate(
            flops=4 * slot_rows * feats * width,
            bytes_accessed=2 * weight_bytes,
            transcendentals=0,
        ),
        name="weight_grads",
    )(rows_t, gate_cot, up_cot)
    return new_gate[None], new_up[None], grad_tokens


def solution(mesh):
    placed = (
        P(("expert", "hid"), "rep"),
        P("rep"),
        P(("expert", "hid"), None),
        P(("expert", "hid"), None),
        P("expert", "rep", "hid"),
        P("expert", "rep", "hid"),
        P("expert", None, "hid"),
        P("expert", None, "hid"),
    )

    def whole(tokens, *rest):
        return jax.shard_map(
            functools.partial(on_device, tokens.shape[1]),
            mesh=mesh,
            in_specs=placed,
            out_specs=(
                P("expert", "rep", "hid"),
                P("expert", "rep", "hid"),
                P(("expert", "hid"), "rep"),
            ),
            check_vma=False,
        )(tokens, *rest)

    return whole
```

time: 73 us -> 45.3 us (0.62)
  Pallas kernels: 0 us -> 38.9 us
  matrix products: 26.5 us -> 0 us
  blocking collectives: 26.3 us -> 0 us
  starting transfers between devices: 10.6 us -> 0 us
  waiting for transfers between devices: 3.69 us -> 0 us
  local copies, waits for them, and re-layouts: 2.3 us -> 5.36 us
  other arithmetic: 1.72 us -> 0 us
  between operations: 1.49 us -> 0.67 us
    pallas_call x0 -> x2, Pallas kernels: none -> 38.9 us  [the longest x1 29.4 us: on_device(): pl.pallas_call(functools.partial(exchange_kernel, (groups, reps, hids, sl...]
    dot_general x6 -> x0, matrix products: 26.5 us -> none  [the longest x1 8.91 us: on_device(): lax.dot_general(up_part, w_up[0], unit_contract, preferred_element_type=j...]
    psum x2 -> x0, blocking collectives: 11.3 us -> none  [feature_total(): return lax.psum(partial_value, 'rep')]
    unnamed x1 -> x0, blocking collectives: 9.9 us -> none
    all_to_all x2 -> x0, starting transfers between devices: 8.42 us -> none  [the longest x1 5.12 us: on_device(): lax.all_to_all(outgoing, 'expert', split_axis=0, concat_axis=0, tiled=True)]
    all_gather x1 -> x0, blocking collectives: 5.03 us -> none  [on_device(): gathered = lax.all_gather(own_rows, 'hid', axis=0, tiled=True)]
    unnamed x21 -> x15, local copies, waits for them, and re-layouts: 0.89 us -> 4.66 us
    all_to_all x2 -> x0, waiting for transfers between devices: 3.69 us -> none  [the longest x1 3.68 us: on_device(): lax.all_to_all(outgoing, 'expert', split_axis=0, concat_axis=0, tiled=True)]
  transfers between devices with their start and end apart: 3 -> 0, of which waited for: 1 -> 0; matrix products, arithmetic and copies ran while one was open for 22% -> 0% of each run, Pallas kernels for 0% -> 0%
where the time goes in v1:
time: 45.3 us; the launch traced here: 45 us
  Pallas kernels  38.9 us (86%)
  local copies, waits for them, and re-layouts  5.36 us (12%)
  between operations  0.67 us (1%)
    pallas_call x1, Pallas kernels, on_device(): pl.pallas_call(functools.partial(exchange_kernel, (groups, reps, hids, sl...  29.4 us
    pallas_call x1, Pallas kernels, on_device(): pl.pallas_call(functools.partial(weight_grad_kernel, chunk, divisor_up_to...  9.57 us
    unnamed x15, local copies, waits for them, and re-layouts  4.66 us

profile of v1, /device:TPU:0, one launch (start us, length us, event | category | flops | bytes accessed | tf_op | source)
XLA Modules:
  0.0 45.0 jit_solution(18212347414770054064)
XLA Ops:
  0.6 0.7 %reshape.9.gain_ref = f32[1,1536]{1,0:T(1,128)S(1)} reshape(f32[1536]{0:T(1024)} %param.9) | data formatting | bytes 12288 | tf_op jit(solution)/shard_map/reshape | solution.py:375
  1.3 0.0 copy-start
  1.3 1.0 %copy-done = bf16[1,40,4096]{2,1,0:T(8,128)(2,1)S(1)} copy-done((bf16[1,40,4096]{2,1,0:T(8,128)(2,1)S(1)}, bf16[1,40,4096]{2,1,0:T(8,128)(2,1)}, u32[]{:S(2)}) %copy-start) | copy-done | bytes 327704
  2.3 0.0 copy-start.2
  2.3 1.0 %copy-done.2 = bf16[1,40,4096]{2,1,0:T(8,128)(2,1)S(1)} copy-done((bf16[1,40,4096]{2,1,0:T(8,128)(2,1)S(1)}, bf16[1,40,4096]{2,1,0:T(8,128)(2,1)}, u32[]{:S(2)}) %copy-start.2) | copy-done | bytes 327704
  3.3 0.0 copy-start.4
  3.3 0.7 %copy-done.4 = bf16[8,1536]{1,0:T(8,128)(2,1)S(1)} copy-done((bf16[8,1536]{1,0:T(8,128)(2,1)S(1)}, bf16[8,1536]{1,0:T(8,128)(2,1)}, u32[]{:S(2)}) %copy-start.4) | copy-done | bytes 24600
  4.0 0.0 copy-start.5
  4.0 0.7 %copy-done.5 = s32[8,2]{0,1:T(2,128)S(1)} copy-done((s32[8,2]{0,1:T(2,128)S(1)}, s32[8,2]{0,1:T(2,128)}, u32[]{:S(2)}) %copy-start.5) | copy-done | bytes 88
  4.7 0.0 copy-start.6
  4.7 0.7 %copy-done.6 = s32[8,2]{0,1:T(2,128)S(1)} copy-done((s32[8,2]{0,1:T(2,128)S(1)}, s32[8,2]{0,1:T(2,128)}, u32[]{:S(2)}) %copy-start.6) | copy-done | bytes 88
  5.4 0.0 copy-start.1
  5.4 0.0 copy-start.3
  5.4 29.4 %rows_and_token_grads.1 = (bf16[1536,40]{1,0:T(8,128)(2,1)S(1)}, bf16[8,1536]{1,0:T(8,128)(2,1)S(1)}) custom-call(bf16[8,1536]{1,0:T(8,128)(2,1)S(1)} %copy-done.4, f32[1,1536]{1,0:T(1,128)S(1)} %reshape.9.gain_ref, s32[2,8]{1,0:T(2,128)S(1)} %bitcast.12, s32[2,8]{1,0:T(2,128)S(1)} %bitcast.13, bf16[1536,4096]{1,0:T(8,128)(2,1)} %bitcast.14, ...), custom_call_target="tpu_custom_call" | custom-call | flops 1610612736 | bytes 25165824 | tf_op jit(solution)/shard_map/rows_and_token_grads/pallas_call | solution.py:335
  34.7 0.0 copy-done.1
  34.8 0.0 copy-done.3
  34.8 9.6 %weight_grads.1 = (bf16[1536,4096]{1,0:T(8,128)(2,1)}, bf16[1536,4096]{1,0:T(8,128)(2,1)}) custom-call(bf16[1536,40]{1,0:T(8,128)(2,1)S(1)} %get-tuple-element.7.rows_t_ref, bf16[40,4096]{1,0:T(8,128)(2,1)S(1)} %bitcast.9, bf16[40,4096]{1,0:T(8,128)(2,1)S(1)} %bitcast.11), custom_call_target="tpu_custom_call" | custom-call | flops 1006632960 | bytes 25165824 | tf_op jit(solution)/shard_map/weight_grads/pallas_call | solution.py:383
  44.4 0.6 %copy.12 = bf16[8,1536]{1,0:T(8,128)(2,1)} copy(bf16[8,1536]{1,0:T(8,128)(2,1)S(1)} %get-tuple-element.16) | data formatting | bytes 49152
Async XLA Ops:
  1.3 1.0 %copy-start = (bf16[1,40,4096]{2,1,0:T(8,128)(2,1)S(1)}, bf16[1,40,4096]{2,1,0:T(8,128)(2,1)}, u32[]{:S(2)}) copy-start(bf16[1,40,4096]{2,1,0:T(8,128)(2,1)} %param.14) | copy-start | bytes 983044
  2.3 1.0 %copy-start.2 = (bf16[1,40,4096]{2,1,0:T(8,128)(2,1)S(1)}, bf16[1,40,4096]{2,1,0:T(8,128)(2,1)}, u32[]{:S(2)}) copy-start(bf16[1,40,4096]{2,1,0:T(8,128)(2,1)} %param.15) | copy-start | bytes 983044
  3.3 0.7 %copy-start.4 = (bf16[8,1536]{1,0:T(8,128)(2,1)S(1)}, bf16[8,1536]{1,0:T(8,128)(2,1)}, u32[]{:S(2)}) copy-start(bf16[8,1536]{1,0:T(8,128)(2,1)} %tokens_ref.1) | copy-start | bytes 73732
  4.0 0.7 %copy-start.5 = (s32[8,2]{0,1:T(2,128)S(1)}, s32[8,2]{0,1:T(2,128)}, u32[]{:S(2)}) copy-start(s32[8,2]{0,1:T(2,128)} %param.10) | copy-start | bytes 196
  4.7 0.7 %copy-start.6 = (s32[8,2]{0,1:T(2,128)S(1)}, s32[8,2]{0,1:T(2,128)}, u32[]{:S(2)}) copy-start(s32[8,2]{0,1:T(2,128)} %param.11) | copy-start | bytes 196
  5.4 29.4 %copy-start.1 = (bf16[1,40,4096]{2,1,0:T(8,128)(2,1)S(1)}, bf16[1,40,4096]{2,1,0:T(8,128)(2,1)}, u32[]{:S(2)}) copy-start(bf16[1,40,4096]{2,1,0:T(8,128)(2,1)} %param.14) | copy-start | bytes 983044
  5.4 29.4 %copy-start.3 = (bf16[1,40,4096]{2,1,0:T(8,128)(2,1)S(1)}, bf16[1,40,4096]{2,1,0:T(8,128)(2,1)}, u32[]{:S(2)}) copy-start(bf16[1,40,4096]{2,1,0:T(8,128)(2,1)} %param.15) | copy-start | bytes 983044
